TPU v7x, 32 devices: a whole 2x2x4 slice. The times are simulated.
32 devices in a mesh: groups: 2 (over y), tile: 4 (over z), col: 2 (over x), branch: 2 (over core).
Axes of the slice: x: 2, y: 2, z: 4, core: 2. Of those that a mesh axis runs over, the one named last changes fastest.
Arguments:
- alignment_tensor: float32 [4, 64, 256, 256], P(('groups', 'branch'), 'tile', 'col'), parts along dimension 0, may hold values from -6 to 6
- residue_grid: float32 [4, 256, 256, 128], P(('groups', 'branch'), 'tile', 'col'), parts along dimension 0, may hold values from -6 to 6
- mixing_scale_vector: float32 [256], replicated, may hold values from 0.1 to 1.9
- logit_offset_scale: float32 [128], replicated, may hold values from 0.1 to 1.9
- feedforward_scale: float32 [256], replicated, may hold values from 0.1 to 1.9
- product_scale_vector: float32 [256], replicated, may hold values from 0.1 to 1.9
- grid_scale_vector: float32 [128], replicated, may hold values from 0.1 to 1.9
- logit_offset_map: float32 [128, 8], replicated, may hold values from -0.5 to 0.5
- asking_mapping: bfloat16 [256, 256], replicated, may hold values from -0.375 to 0.375
- lookup_mapping: bfloat16 [256, 256], replicated, may hold values from -0.375 to 0.375
- content_mapping: bfloat16 [256, 256], replicated, may hold values from -0.375 to 0.375
- mixing_return_matrix: bfloat16 [256, 256], replicated, may hold values from -0.375 to 0.375
- alignment_widen_map: bfloat16 [256, 1024], replicated, may hold values from -0.375 to 0.375
- alignment_shrink_map: bfloat16 [1024, 256], replicated, may hold values from -0.1875 to 0.1875
- former_embedding_map: bfloat16 [256, 32], replicated, may hold values from -0.375 to 0.375
- latter_embedding_map: bfloat16 [256, 32], replicated, may hold values from -0.375 to 0.375
- product_return_map: float32 [1024, 128], replicated, may hold values from -1 to 1
- grid_widen_map: bfloat16 [128, 512], replicated, may hold values from -0.5 to 0.5
- grid_shrink_map: bfloat16 [512, 128], replicated, may hold values from -0.25 to 0.25
Outputs:
- alignment_revised: float32 [4, 64, 256, 256], P(('groups', 'branch'), 'tile', 'col'), parts along dimension 0
- grid_revised: float32 [4, 256, 256, 128], P(('groups', 'branch'), 'tile', 'col'), parts along dimension 0
There are 2 independent parts, one for each index of `groups`. A program takes and returns all parts, laid end to end along the dimension named above; an argument that names none is the same for every part. Nothing has to cross between parts.
All inputs are finite; a program needn't handle non-finite values.
Results may differ from a plain program's by a relative error of at most 0.0075.
Values may be sent and summed in bfloat16 or wider, within the bound.
A program may use at most 128 MiB of HBM per device.

v0:
```python
import jax
import jax.numpy as jnp
from jax import lax
from jax.sharding import PartitionSpec as P

SEQUENCE_DEPTH = 64


def standardize_features(x, gain):
    mean = jnp.mean(x, axis=-1, keepdims=True)
    var = jnp.mean((x - mean) ** 2, axis=-1, keepdims=True)
    return (x - mean) * lax.rsqrt(var + 1e-05) * gain


def on_device(
    alignment_tensor,
    residue_grid,
    mixing_scale_vector,
    logit_offset_scale,
    feedforward_scale,
    product_scale_vector,
    grid_scale_vector,
    logit_offset_map,
    asking_mapping,
    lookup_mapping,
    content_mapping,
    mixing_return_matrix,
    alignment_widen_map,
    alignment_shrink_map,
    former_embedding_map,
    latter_embedding_map,
    product_return_map,
    grid_widen_map,
    grid_shrink_map,
):
    sample_alignment = alignment_tensor[0]
    local_pair = residue_grid[0]
    subspace_total = logit_offset_map.shape[1]
    feature_extent = sample_alignment.shape[-1]
    subspace_number = feature_extent // subspace_total
    sequences_available = sample_alignment.shape[0]
    chain_available = sample_alignment.shape[1]
    tile_rows = local_pair.shape[0]
    tile_cols = local_pair.shape[1]
    product_extent = former_embedding_map.shape[1]
    product_operands = standardize_features(sample_alignment, product_scale_vector).astype(
        jnp.bfloat16
    )
    former_tensor = jnp.dot(
        product_operands, former_embedding_map, preferred_element_type=jnp.float32
    ).astype(jnp.bfloat16)
    latter_tensor = jnp.dot(
        product_operands, latter_embedding_map, preferred_element_type=jnp.float32
    ).astype(jnp.bfloat16)
    left_rows, right_rows = (
        lax.all_gather(former_tensor, "tile", axis=0, tiled=True),
        lax.all_gather(latter_tensor, "tile", axis=0, tiled=True),
    )
    left_all = lax.all_gather(left_rows, "col", axis=1, tiled=True)
    left_mine = lax.dynamic_slice_in_dim(left_all, lax.axis_index("tile") * tile_rows, tile_rows, 1)
    tensor_product = (
        jnp.einsum("era,eyq->ryaq", left_mine, right_rows, preferred_element_type=jnp.float32)
        / SEQUENCE_DEPTH
    )
    update = jnp.dot(
        tensor_product.reshape(tile_rows, tile_cols, product_extent * product_extent),
        product_return_map,
        precision=lax.Precision.HIGHEST,
    )
    bias_tile = jnp.einsum(
        "ijc,ch->hij",
        standardize_features(local_pair, logit_offset_scale),
        logit_offset_map,
        precision=lax.Precision.HIGHEST,
    )
    wide = lax.all_gather(bias_tile, "col", axis=2, tiled=True)
    whole = lax.all_gather(wide.astype(jnp.bfloat16), "tile", axis=1, tiled=True).astype(wide.dtype)
    bias = lax.dynamic_slice_in_dim(
        whole, lax.axis_index("col") * chain_available, chain_available, 1
    )
    standardized_source = standardize_features(sample_alignment, mixing_scale_vector).astype(
        jnp.bfloat16
    )
    asking_vectors = jnp.dot(
        standardized_source, asking_mapping, preferred_element_type=jnp.float32
    ).astype(jnp.bfloat16)
    lookup_vectors = jnp.dot(
        standardized_source, lookup_mapping, preferred_element_type=jnp.float32
    ).astype(jnp.bfloat16)
    content_vectors = jnp.dot(
        standardized_source, content_mapping, preferred_element_type=jnp.float32
    ).astype(jnp.bfloat16)
    all_keys, all_values = (
        lax.all_gather(lookup_vectors, "col", axis=1, tiled=True),
        lax.all_gather(content_vectors, "col", axis=1, tiled=True),
    )
    total_res = all_keys.shape[1]
    asking_vectors = asking_vectors.reshape(
        sequences_available, chain_available, subspace_total, subspace_number
    )
    all_keys = all_keys.reshape(sequences_available, total_res, subspace_total, subspace_number)
    all_values = all_values.reshape(sequences_available, total_res, subspace_total, subspace_number)
    scores = (
        jnp.einsum("sqhd,skhd->shqk", asking_vectors, all_keys, preferred_element_type=jnp.float32)
        / jnp.sqrt(jnp.float32(subspace_number))
        + bias[None]
    )
    weights = jax.nn.softmax(scores, axis=-1).astype(jnp.bfloat16)
    mixing_outcome = jnp.einsum(
        "shqk,skhd->sqhd", weights, all_values, preferred_element_type=jnp.float32
    )
    mixing_outcome = mixing_outcome.astype(jnp.bfloat16).reshape(
        sequences_available, chain_available, feature_extent
    )
    alignment_activations = sample_alignment + jnp.dot(
        mixing_outcome, mixing_return_matrix, preferred_element_type=jnp.float32
    )
    expanded_features = jax.nn.relu(
        jnp.dot(
            standardize_features(alignment_activations, feedforward_scale).astype(jnp.bfloat16),
            alignment_widen_map,
            preferred_element_type=jnp.float32,
        )
    ).astype(jnp.bfloat16)
    alignment_revised = alignment_activations + jnp.dot(
        expanded_features, alignment_shrink_map, preferred_element_type=jnp.float32
    )
    pair_mid = local_pair + update
    spread = jax.nn.relu(
        jnp.dot(
            standardize_features(pair_mid, grid_scale_vector).astype(jnp.bfloat16),
            grid_widen_map,
            preferred_element_type=jnp.float32,
        )
    ).astype(jnp.bfloat16)
    grid_revised = pair_mid + jnp.dot(spread, grid_shrink_map, preferred_element_type=jnp.float32)
    return (alignment_revised[None], grid_revised[None])


def solution(mesh):
    placed = (
        P(("groups", "branch"), "tile", "col", None),
        P(("groups", "branch"), "tile", "col", None),
        P(),
        P(),
        P(),
        P(),
        P(),
        P(),
        P(),
        P(),
        P(),
        P(),
        P(),
        P(),
        P(),
        P(),
        P(),
        P(),
        P(),
    )
    return jax.shard_map(
        on_device,
        mesh=mesh,
        in_specs=placed,
        out_specs=(
            P(("groups", "branch"), "tile", "col", None),
            P(("groups", "branch"), "tile", "col", None),
        ),
        check_vma=False,
    )
```

profile of v0, /device:TPU:8, one launch (start us, length us, event | category | flops | bytes accessed | tf_op | source)
XLA Modules:
  0.0 220.7 jit_solution(14404370128680419553)
XLA Ops:
  7.3 2.1 reduce_sum.89
  9.4 2.2 %multiply_reduce_fusion.3 = f32[16,128]{1,0:T(8,128)S(1)} fusion(f32[1,16,128,256]{3,2,1,0:T(8,128)} %param.19, f32[16,128]{1,0:T(8,128)S(1)} %broadcast_multiply_fusion.3), kind=kLoop, calls=%fused_computation.38 | loop fusion | flops 1570816 | bytes 2113536 | tf_op jit(solution)/shard_map/reduce_sum | solution.py:11
  12.6 16.5 %all_gather.26 = bf16[64,128,32]{1,2,0:T(8,128)(2,1)S(1)} all-gather(bf16[16,128,32]{1,2,0:T(8,128)(2,1)S(1)} %convolution_convert_fusion.3), channel_id=1, replica_groups=mesh['groups'=2,'tile'=4,'col'=2,'branch'=2] {'tile'}, dimensions={0}, use_global_device_ids=true | all-gather | bytes 655360 | tf_op jit(solution)/shard_map/all_gather | solution.py:56
  29.1 1.6 copy.65
  30.8 5.6 %copy.61 = f32[1,64,128,128]{2,3,1,0:T(8,128)} copy(f32[1,64,128,128]{3,2,1,0:T(8,128)} %param.20) | data formatting | bytes 8388608 | tf_op args[1]
  36.4 3.5 %reduce_sum.91 = f32[64,128]{1,0:T(8,128)S(1)} reduce(f32[1,64,128,128]{3,2,1,0:T(8,128)} %param.20, f32[]{:T(128)} %constant.17.clone.1), dimensions={0,3}, to_apply=%region_2.0 | reduce | flops 1040384 | bytes 4227076 | tf_op jit(solution)/shard_map/reduce_sum | solution.py:10
  39.9 3.5 %multiply_reduce_fusion.1 = f32[64,128]{1,0:T(8,128)S(1)} fusion(f32[1,64,128,128]{2,3,1,0:T(8,128)} %copy.61, f32[64,128]{1,0:T(8,128)S(1)} %broadcast_multiply_fusion.1), kind=kLoop, calls=%fused_computation.21 | loop fusion | flops 3137536 | bytes 4259840 | tf_op jit(solution)/shard_map/reduce_sum | solution.py:11
  43.7 2.7 %fusion.26 = bf16[8,64,128]{2,0,1:T(8,128)(2,1)S(1)} fusion(f32[1,64,128,128]{2,3,1,0:T(8,128)S(1)} %copy-done.3, f32[128]{0:T(128)S(1)} %copy-done.18, f32[64,128]{1,0:T(8,128)S(1)} %add_rsqrt_fusion.1, f32[64,128]{1,0:T(8,128)S(1)} %broadcast_multiply_fusion.1, f32[128,8]{0,1:T(8,128)S(1)} %copy-done.15), kind=kOutput, calls=%fused_computation.44 | convolution fusion | flops 103809024 | bytes 4395520 | tf_op jit(solution)/shard_map/ijc,ch->hij/dot_general | solution.py:70
  46.5 8.6 %all_gather.23 = bf16[8,64,256]{2,0,1:T(8,128)(2,1)} all-gather(bf16[8,64,128]{2,0,1:T(8,128)(2,1)S(1)} %fusion.26), channel_id=1, replica_groups=mesh['groups'=2,'tile'=4,'col'=2,'branch'=2] {'col'}, dimensions={2}, use_global_device_ids=true | all-gather | bytes 393216 | tf_op jit(solution)/shard_map/all_gather | solution.py:76
  58.4 2.6 %convolution_convert_fusion.2 = bf16[16,128,256]{2,1,0:T(8,128)(2,1)} fusion(bf16[16,128,256]{2,1,0:T(8,128)(2,1)} %copy-done.4, bf16[256,256]{1,0:T(8,128)(2,1)S(1)} %copy-done.9), kind=kOutput, calls=%fused_computation.43 | convolution fusion | flops 268959744 | bytes 2228224 | tf_op jit(solution)/shard_map/dot_general | solution.py:90
  62.1 16.4 %all_gather.25 = bf16[64,128,32]{1,2,0:T(8,128)(2,1)S(1)} all-gather(bf16[16,128,32]{1,2,0:T(8,128)(2,1)S(1)} %convolution_convert_fusion.4), channel_id=1, replica_groups=mesh['groups'=2,'tile'=4,'col'=2,'branch'=2] {'tile'}, dimensions={0}, use_global_device_ids=true | all-gather | bytes 655360 | tf_op jit(solution)/shard_map/all_gather | solution.py:57
  78.4 2.7 %convolution_convert_fusion.1 = bf16[16,128,256]{2,1,0:T(8,128)(2,1)} fusion(bf16[16,128,256]{2,1,0:T(8,128)(2,1)} %copy-done.4, bf16[256,256]{1,0:T(8,128)(2,1)S(1)} %copy-done.10), kind=kOutput, calls=%fused_computation.42 | convolution fusion | flops 268959744 | bytes 2228224 | tf_op jit(solution)/shard_map/dot_general | solution.py:84
  81.1 2.3 %copy.59 = bf16[16,128,256]{1,2,0:T(8,128)(2,1)} copy(bf16[16,128,256]{2,1,0:T(8,128)(2,1)} %convolution_convert_fusion.1) | data formatting | bytes 2097152 | tf_op jit(solution)/shard_map/convert_element_type | solution.py:86
  83.4 14.2 %multiply_bitcast_fusion = f32[64,128,32,32]{1,0,2,3:T(8,128)} fusion(bf16[64,128,32,1]{1,2,0,3:T(8,128)(2,1)S(1)} %bitcast.95, bf16[64,256,32]{0,1,2:T(8,128)(2,1)} %all-gather.11.cloned.1.call-done, s32[]{:T(128)S(6)} %select_n.7), kind=kOutput, calls=%fused_computation.1 | convolution fusion | flops 1082130432 | bytes 34603012 | tf_op jit(solution)/shard_map/era,eyq->ryaq/dot_general | solution.py:62
  97.7 32.0 %copy.67 = f32[64,128,32,32]{1,3,2,0:T(8,128)} copy(f32[64,128,32,32]{1,0,2,3:T(8,128)} %multiply_bitcast_fusion) | data formatting | bytes 67108864 | tf_op jit(solution)/shard_map/div | solution.py:62
  129.7 25.6 %fusion.58 = (f32[64,128]{1,0:T(8,128)S(1)}, f32[64,128,128]{1,2,0:T(8,128)}) fusion(f32[64,128,1024]{1,2,0:T(8,128)} %bitcast.94, f32[1024,128]{1,0:T(8,128)S(1)} %copy-done, f32[1,64,128,128]{2,3,1,0:T(8,128)} %copy.61), kind=kOutput, calls=%fused_computation.80 | convolution fusion | flops 12886990848 | bytes 42500096 | tf_op jit(solution)/shard_map/dot_general | solution.py:65
  155.3 3.0 %multiply_reduce_fusion = f32[64,128]{1,0:T(8,128)S(1)} fusion(f32[64,128,128]{1,2,0:T(8,128)} %get-tuple-element.15, f32[64,128]{1,0:T(8,128)S(1)} %broadcast_multiply_fusion), kind=kLoop, calls=%fused_computation.16 | loop fusion | flops 3137536 | bytes 4259840 | tf_op jit(solution)/shard_map/reduce_sum | solution.py:11
  158.4 10.1 %add_bitcast_fusion = f32[1,64,128,128]{2,3,1,0:T(8,128)} fusion(f32[64,128,128]{1,2,0:T(8,128)} %get-tuple-element.15, f32[128]{0:T(128)S(1)} %copy-done.17, f32[64,128]{1,0:T(8,128)S(1)} %add_rsqrt_fusion, f32[64,128]{1,0:T(8,128)S(1)} %broadcast_multiply_fusion, bf16[512,128]{1,0:T(8,128)(2,1)S(1)} %copy-done.6, bf16[128,512]{1,0:T(8,128)(2,1)S(1)} %copy-done.7), kind=kOutput, calls=%fused_computation.14 | convolution fusion | flops 2161115136 | bytes 8716800 | tf_op jit(solution)/shard_map/dot_general | solution.py:136
  168.5 5.6 %copy.72 = f32[1,64,128,128]{3,2,1,0:T(8,128)} copy(f32[1,64,128,128]{2,3,1,0:T(8,128)} %add_bitcast_fusion) | data formatting | bytes 8388608
  176.6 3.9 %copy.60 = bf16[16,256,256]{1,2,0:T(8,128)(2,1)} copy(bf16[16,256,256]{2,1,0:T(8,128)(2,1)} %all-gather.7.cloned.1.call-done) | data formatting | bytes 4194304 | tf_op jit(solution)/shard_map/all_gather | solution.py:94
  180.5 12.4 %fusion.56 = (f32[16,8,128]{2,1,0:T(8,128)S(1)}, f32[16,8,128,256]{3,2,1,0:T(8,128)}) fusion(f32[8,128,256]{2,1,0:T(8,128)} %copy.63, bf16[16,128,8,32]{1,3,2,0:T(8,128)(2,1)} %bitcast.98, bf16[16,256,8,32]{1,3,2,0:T(8,128)(2,1)} %bitcast.96), kind=kOutput, calls=%fused_computation.78 | convolution fusion | flops 285212928 | bytes 21037056 | tf_op jit(solution)/shard_map/sub | solution.py:108
  192.8 3.9 %copy.58 = bf16[16,256,256]{1,2,0:T(8,128)(2,1)} copy(bf16[16,256,256]{2,1,0:T(8,128)(2,1)} %all-gather.5.cloned.1.call-done) | data formatting | bytes 4194304 | tf_op jit(solution)/shard_map/all_gather | solution.py:95
  196.7 8.3 %fusion.25 = bf16[16,8,32,128]{3,2,1,0:T(8,128)(2,1)S(1)} fusion(bf16[16,256,8,32]{1,3,2,0:T(8,128)(2,1)} %bitcast.97, f32[16,8,128,256]{3,2,1,0:T(8,128)} %get-tuple-element.11, f32[16,8,128]{2,1,0:T(8,128)S(1)} %get-tuple-element.10), kind=kOutput, calls=%fused_computation.40 | convolution fusion | flops 277348352 | bytes 19988480 | tf_op jit(solution)/shard_map/shqk,skhd->sqhd/dot_general | solution.py:109
  207.9 6.3 %add_bitcast_fusion.1 = f32[1,16,128,256]{3,2,1,0:T(8,128)} fusion(f32[16,128,256]{2,1,0:T(8,128)} %copy-done.5, f32[256]{0:T(256)S(1)} %copy-done.20, f32[16,128]{1,0:T(8,128)S(1)} %add_rsqrt_fusion.2, f32[16,128]{1,0:T(8,128)S(1)} %broadcast_multiply_fusion.2, bf16[1024,256]{1,0:T(8,128)(2,1)S(1)} %copy-done.19, bf16[256,1024]{1,0:T(8,128)(2,1)} %param.31), kind=kOutput, calls=%fused_computation.31 | convolution fusion | flops 2154299392 | bytes 5260288 | tf_op jit(solution)/shard_map/dot_general | solution.py:125
  (70 shorter events, 10.9 us)
Async XLA Ops:
  7.2 122.5 %copy-start = (f32[1024,128]{1,0:T(8,128)S(1)}, f32[1024,128]{1,0:T(8,128)}, u32[]{:S(2)}) copy-start(f32[1024,128]{1,0:T(8,128)} %param.35) | copy-start | bytes 1572868
  7.2 4.4 %copy-start.2 = (f32[1,16,128,256]{3,2,1,0:T(8,128)S(1)}, f32[1,16,128,256]{3,2,1,0:T(8,128)}, u32[]{:S(2)}) copy-start(f32[1,16,128,256]{3,2,1,0:T(8,128)} %param.19) | copy-start | bytes 6291460
  7.2 4.4 %copy-start.14 = (f32[256]{0:T(256)S(1)}, f32[256]{0:T(256)}, u32[]{:S(2)}) copy-start(f32[256]{0:T(256)} %param.24) | copy-start | bytes 3076
  7.2 4.4 %copy-start.12 = (bf16[256,32]{0,1:T(8,128)(2,1)S(1)}, bf16[256,32]{0,1:T(8,128)(2,1)}, u32[]{:S(2)}) copy-start(bf16[256,32]{0,1:T(8,128)(2,1)} %param.33) | copy-start | bytes 49156
  7.2 76.2 %all-gather.11.cloned.1.call-start = ((), (), s32[]{:S(2)}) async-start(), calls=%async_computation.3 | async-start | bytes 3145728 | tf_op jit(solution)/shard_map/all_gather | solution.py:59
  30.7 143.4 %all-gather.9.cloned.1.call-start = ((), (), s32[]{:S(2)}) async-start(), calls=%async_computation.2 | async-start | bytes 1310720 | tf_op jit(solution)/shard_map/all_gather | solution.py:77
  36.4 7.1 %copy-start.15 = (f32[128,8]{0,1:T(8,128)S(1)}, f32[128,8]{0,1:T(8,128)}, u32[]{:S(2)}) copy-start(f32[128,8]{0,1:T(8,128)} %param.26) | copy-start | bytes 12292
  36.4 7.1 %copy-start.18 = (f32[128]{0:T(128)S(1)}, f32[128]{0:T(128)}, u32[]{:S(2)}) copy-start(f32[128]{0:T(128)} %param.22) | copy-start | bytes 1540
  39.9 3.9 %copy-start.3 = (f32[1,64,128,128]{2,3,1,0:T(8,128)S(1)}, f32[1,64,128,128]{2,3,1,0:T(8,128)}, u32[]{:S(2)}) copy-start(f32[1,64,128,128]{2,3,1,0:T(8,128)} %copy.61) | copy-start | bytes 12582916
  39.9 15.3 %copy-start.16 = (f32[256]{0:T(256)S(1)}, f32[256]{0:T(256)}, u32[]{:S(2)}) copy-start(f32[256]{0:T(256)} %param.21) | copy-start | bytes 3076
  43.4 13.5 %copy-start.8 = (bf16[256,256]{1,0:T(8,128)(2,1)S(1)}, bf16[256,256]{1,0:T(8,128)(2,1)}, u32[]{:S(2)}) copy-start(bf16[256,256]{1,0:T(8,128)(2,1)} %param.28) | copy-start | bytes 393220
  46.5 12.0 %copy-start.9 = (bf16[256,256]{1,0:T(8,128)(2,1)S(1)}, bf16[256,256]{1,0:T(8,128)(2,1)}, u32[]{:S(2)}) copy-start(bf16[256,256]{1,0:T(8,128)(2,1)} %param.29) | copy-start | bytes 393220
  55.1 6.0 %copy-start.13 = (bf16[256,32]{0,1:T(8,128)(2,1)S(1)}, bf16[256,32]{0,1:T(8,128)(2,1)}, u32[]{:S(2)}) copy-start(bf16[256,32]{0,1:T(8,128)(2,1)} %param.34) | copy-start | bytes 49156
  55.1 121.4 %all-gather.7.cloned.1.call-start = ((), (), s32[]{:S(2)}) async-start(), calls=%async_computation.1 | async-start | bytes 3145728 | tf_op jit(solution)/shard_map/all_gather | solution.py:94
  58.4 20.1 %copy-start.10 = (bf16[256,256]{1,0:T(8,128)(2,1)S(1)}, bf16[256,256]{1,0:T(8,128)(2,1)}, u32[]{:S(2)}) copy-start(bf16[256,256]{1,0:T(8,128)(2,1)} %param.27) | copy-start | bytes 393220
  58.4 134.4 %all-gather.5.cloned.1.call-start = ((), (), s32[]{:S(2)}) async-start(), calls=%async_computation | async-start | bytes 3145728 | tf_op jit(solution)/shard_map/all_gather | solution.py:95
  155.3 3.1 %copy-start.6 = (bf16[512,128]{1,0:T(8,128)(2,1)S(1)}, bf16[512,128]{1,0:T(8,128)(2,1)}, u32[]{:S(2)}) copy-start(bf16[512,128]{1,0:T(8,128)(2,1)} %param.37) | copy-start | bytes 393220
  155.3 3.1 %copy-start.7 = (bf16[128,512]{1,0:T(8,128)(2,1)S(1)}, bf16[128,512]{1,0:T(8,128)(2,1)}, u32[]{:S(2)}) copy-start(bf16[128,512]{1,0:T(8,128)(2,1)} %param.36) | copy-start | bytes 393220
  155.3 3.1 %copy-start.17 = (f32[128]{0:T(128)S(1)}, f32[128]{0:T(128)}, u32[]{:S(2)}) copy-start(f32[128]{0:T(128)} %param.25) | copy-start | bytes 1540
  196.7 8.4 %copy-start.11 = (bf16[256,256]{1,0:T(8,128)(2,1)S(1)}, bf16[256,256]{1,0:T(8,128)(2,1)}, u32[]{:S(2)}) copy-start(bf16[256,256]{1,0:T(8,128)(2,1)} %param.30) | copy-start | bytes 393220
  205.1 2.8 %copy-start.19 = (bf16[1024,256]{1,0:T(8,128)(2,1)S(1)}, bf16[1024,256]{1,0:T(8,128)(2,1)}, u32[]{:S(2)}) copy-start(bf16[1024,256]{1,0:T(8,128)(2,1)} %param.32) | copy-start | bytes 1572868
  205.1 2.8 %copy-start.20 = (f32[256]{0:T(256)S(1)}, f32[256]{0:T(256)}, u32[]{:S(2)}) copy-start(f32[256]{0:T(256)} %param.23) | copy-start | bytes 3076
  205.9 1.4 copy-start.5
  207.9 6.3 %copy-start.1 = (f32[1024,128]{1,0:T(8,128)S(1)}, f32[1024,128]{1,0:T(8,128)}, u32[]{:S(2)}) copy-start(f32[1024,128]{1,0:T(8,128)} %param.35) | copy-start | bytes 1572868
  (1 other events, 1.0 us)
Sparse Core Ops, SparseCore 0:
  30.8 37.0 all-gather.10
  69.5 27.9 all-gather.8
  99.0 32.6 all-gather.6
  133.0 33.1 all-gather.4
where the time goes:
time: 223 us; the launch traced here: 221 us
  matrix products  89.1 us (40%)
  local copies, waits for them, and re-layouts  58.9 us (26%)
  blocking collectives  41.5 us (19%)
  other arithmetic  16.9 us (8%)
  between operations  14.1 us (6%)
    div x1, local copies, waits for them, and re-layouts, on_device(): jnp.einsum('era,eyq->ryaq', left_mine, right_rows, preferred_element_type...  32 us
    dot_general x1, matrix products, on_device(): jnp.dot(tensor_product.reshape(tile_rows, tile_cols, product_extent * pro...  25.6 us
    all_gather x1, blocking collectives, on_device(): lax.all_gather(former_tensor, 'tile', axis=0, tiled=True)  16.5 us
    all_gather x1, blocking collectives, on_device(): lax.all_gather(latter_tensor, 'tile', axis=0, tiled=True)  16.4 us
    dot_general x1, matrix products, on_device(): jnp.einsum('era,eyq->ryaq', left_mine, right_rows, preferred_element_type...  14.2 us
    unnamed x44, local copies, waits for them, and re-layouts  13.9 us
    sub x1, matrix products, on_device(): weights = jax.nn.softmax(scores, axis=-1).astype(jnp.bfloat16)  12.4 us
    dot_general x1, matrix products, on_device(): jnp.dot(spread, grid_shrink_map, preferred_element_type=jnp.float32)  10.1 us
  transfers between devices with their start and end apart: 4, of which 0 were waited for; matrix products, arithmetic and copies ran while one was open for 61% of the time, Pallas kernels for 0%

commit v1 on v0

--- a/solution.py
+++ b/solution.py
@@ -1,6 +1,10 @@
+import functools
+
 import jax
 import jax.numpy as jnp
 from jax import lax
+from jax.experimental import pallas as pl
+from jax.experimental.pallas import tpu as pltpu
 from jax.sharding import PartitionSpec as P
 
 SEQUENCE_DEPTH = 64
@@ -12,7 +16,7 @@
     return (x - mean) * lax.rsqrt(var + 1e-05) * gain
 
 
-def on_device(
+def plain_device(
     alignment_tensor,
     residue_grid,
     mixing_scale_vector,
@@ -137,6 +141,453 @@
     return (alignment_revised[None], grid_revised[None])
 
 
+BF = jnp.bfloat16
+F32 = jnp.float32
+LANES = 128
+LOG2E = 1.4426950408889634
+MESH = pl.DeviceIdType.MESH
+
+
+def center(x):
+    mean = jnp.mean(x, axis=-1, keepdims=True)
+    d = x - mean
+    return d * lax.rsqrt(jnp.mean(d * d, axis=-1, keepdims=True) + 1e-05)
+
+
+def dot(a, b, ca=1, cb=0):
+    return lax.dot_general(a, b, (((ca,), (cb,)), ((), ())), preferred_element_type=F32)
+
+
+def exchange_kernel(
+    tiles,
+    cols,
+    x_ref,
+    pair_ref,
+    gm_ref,
+    gp_ref,
+    gb_ref,
+    mapt_ref,
+    wlt_ref,
+    wrt_ref,
+    normed_ref,
+    left_ref,
+    right_ref,
+    bias_ref,
+    y_ref,
+    lmine,
+    bmine,
+    wl4,
+    send_x,
+    recv_x,
+    send_l,
+    recv_l,
+    send_r,
+    recv_r,
+    send_b,
+    recv_b,
+):
+    t = lax.axis_index("tile")
+    c = lax.axis_index("col")
+    n = tiles // cols
+    rows, res, feat = x_ref.shape
+    trows, tcols, cz = pair_ref.shape
+    prod = wlt_ref.shape[0]
+    pack = LANES // prod
+    barrier = pltpu.get_barrier_semaphore()
+    for dt in range(tiles):
+        for dc in range(cols):
+            if dt or dc:
+                pl.semaphore_signal(
+                    barrier,
+                    inc=1,
+                    device_id={
+                        "tile": lax.rem(t + dt, tiles),
+                        "col": lax.rem(c + dc, cols),
+                    },
+                    device_id_type=MESH,
+                )
+
+    wlt = wlt_ref[...]
+    wl4[...] = jnp.zeros_like(wl4)
+    for r in range(pack):
+        wl4[r, r * prod : (r + 1) * prod, :] = wlt
+    gp = gp_ref[...]
+    gm = gm_ref[...]
+    own = normed_ref.at[c]
+    chunks = feat // LANES
+
+    def factor(w, s, at):
+        parts = [y_ref[(f, s) + at].astype(BF) for f in range(chunks)]
+        return dot(w, jnp.concatenate(parts, axis=1), 1, 1)
+
+    def rows_body(s, carry):
+        z = center(x_ref[s])
+        y = z * gp
+        for f in range(chunks):
+            y_ref[f, s, :, :] = y[:, f * LANES : (f + 1) * LANES]
+        own[s, :, :] = (z * gm).astype(BF)
+        return carry
+
+    lax.fori_loop(0, rows, rows_body, 0)
+
+    group = 16
+    for s0 in range(0, rows, group):
+        right = jnp.stack(
+            [factor(wrt_ref[...], s, ()) for s in range(s0, s0 + group)]
+        )
+        right_ref[t, :, s0 : s0 + group, :] = jnp.swapaxes(right, 0, 1).astype(BF)
+        left = []
+        for s in range(s0, s0 + group):
+            acc = None
+            for r in range(pack):
+                at = (pl.ds(r, res // pack, stride=pack), slice(None))
+                parts = [y_ref[(f, s) + at].astype(BF) for f in range(chunks)]
+                part = dot(jnp.concatenate(parts, axis=1), wl4[r], 1, 1)
+                acc = part if acc is None else acc + part
+            left.append(acc)
+        lmine[:, s0 : s0 + group, :] = jnp.swapaxes(jnp.stack(left), 0, 1).astype(BF)
+
+    pl.semaphore_wait(barrier, tiles * cols - 1)
+
+    piece = trows // pack
+
+    def left_copy(k, c2):
+        dest = c * n + k
+        src = lmine.at[pl.ds(k * piece, piece)]
+        i = k * cols + c2
+        away = jnp.logical_or(dest != t, c != c2)
+        remote = pltpu.make_async_remote_copy(
+            src_ref=src,
+            dst_ref=left_ref.at[t],
+            send_sem=send_l.at[i],
+            recv_sem=recv_l.at[t],
+            device_id={"tile": dest, "col": c2},
+            device_id_type=MESH,
+        )
+        local = pltpu.make_async_copy(src, left_ref.at[t], recv_l.at[t])
+        return away, remote, local
+
+    def bias_copy(t2):
+        owner = t // n
+        slot = bias_ref.at[lax.rem(t, n), c]
+        sem = recv_b.at[lax.rem(t, n) * cols + c]
+        away = jnp.logical_or(t2 != t, c != owner)
+        remote = pltpu.make_async_remote_copy(
+            src_ref=bmine,
+            dst_ref=slot,
+            send_sem=send_b.at[t2],
+            recv_sem=sem,
+            device_id={"tile": t2, "col": owner},
+            device_id_type=MESH,
+        )
+        local = pltpu.make_async_copy(bmine, slot, sem)
+        return away, remote, local
+
+    def start(copy):
+        away, remote, local = copy
+
+        @pl.when(away)
+        def _():
+            remote.start()
+
+        @pl.when(jnp.logical_not(away))
+        def _():
+            local.start()
+
+    def finish(copy):
+        away, remote, _ = copy
+
+        @pl.when(away)
+        def _():
+            remote.wait_send()
+
+    def right_copy(dt):
+        return pltpu.make_async_remote_copy(
+            src_ref=right_ref.at[t],
+            dst_ref=right_ref.at[t],
+            send_sem=send_r.at[dt],
+            recv_sem=recv_r.at[t],
+            device_id={"tile": lax.rem(t + dt, tiles)},
+            device_id_type=MESH,
+        )
+
+    def normed_copy(dc):
+        return pltpu.make_async_remote_copy(
+            src_ref=own,
+            dst_ref=own,
+            send_sem=send_x.at[dc],
+            recv_sem=recv_x.at[c],
+            device_id={"col": lax.rem(c + dc, cols)},
+            device_id_type=MESH,
+        )
+
+    lefts = [left_copy(k, c2) for k in range(n) for c2 in range(cols)]
+    for copy in lefts:
+        start(copy)
+    for dt in range(1, tiles):
+        right_copy(dt).start()
+    for dc in range(1, cols):
+        normed_copy(dc).start()
+
+    mapt = mapt_ref[...] * gb_ref[...]
+    high = mapt.astype(BF)
+    low = (mapt - high.astype(F32)).astype(BF)
+    both = jnp.concatenate([high.astype(F32), low.astype(F32)], axis=0).astype(BF)
+    heads = mapt.shape[0]
+    ib = 16
+
+    def bias_body(b, carry):
+        z = center(pair_ref[pl.ds(b * ib, ib)]).astype(BF)
+        out = []
+        for i in range(ib):
+            p = dot(both, z[i], 1, 1)
+            out.append(p[:heads] + p[heads:])
+        bmine[:, pl.ds(pl.multiple_of(b * ib, ib), ib), :] = jnp.swapaxes(
+            jnp.stack(out), 0, 1
+        ).astype(BF)
+        return carry
+
+    lax.fori_loop(0, trows // ib, bias_body, 0)
+    biases = [bias_copy(t2) for t2 in range(tiles)]
+    for copy in biases:
+        start(copy)
+
+    def arrived(ref, sem):
+        pltpu.make_async_copy(ref, ref, sem).wait()
+
+    for t2 in range(tiles):
+        arrived(left_ref.at[t2], recv_l.at[t2])
+    for dt in range(1, tiles):
+        src = lax.rem(t + dt, tiles)
+        arrived(right_ref.at[src], recv_r.at[src])
+    for dc in range(1, cols):
+        src = lax.rem(c + dc, cols)
+        arrived(normed_ref.at[src], recv_x.at[src])
+    for k in range(n):
+        for c2 in range(cols):
+            arrived(bias_ref.at[k, c2], recv_b.at[k * cols + c2])
+    for copy in lefts:
+        finish(copy)
+    for dt in range(1, tiles):
+        right_copy(dt).wait_send()
+    for dc in range(1, cols):
+        normed_copy(dc).wait_send()
+    for copy in biases:
+        finish(copy)
+
+
+def pair_kernel(
+    depth,
+    left_ref,
+    right_ref,
+    pair_ref,
+    wp_ref,
+    g_ref,
+    widen_ref,
+    shrink_ref,
+    out_ref,
+    rmat,
+    wmat,
+):
+    tiles, prod, rows, tcols = right_ref.shape
+    cz = pair_ref.shape[-1]
+    pack = pair_ref.shape[0]
+
+    @pl.when(pl.program_id(0) == 0)
+    def _():
+        for d in range(prod):
+            for t in range(tiles):
+                rmat[t * rows : (t + 1) * rows, d * tcols : (d + 1) * tcols] = right_ref[t, d]
+        step = LANES // prod
+        for d0 in range(0, prod, step):
+            w = jnp.concatenate(
+                [wp_ref[pl.ds(d, prod, stride=prod), :] for d in range(d0, d0 + step)], axis=0
+            )
+            wmat[:, d0 * prod : (d0 + step) * prod] = (w.T * (1.0 / depth)).astype(BF)
+
+    left = jnp.concatenate([left_ref[t, 0] for t in range(tiles)], axis=0)
+    left = left.astype(F32).T.astype(BF)
+    dn = 8
+    total = None
+    for d0 in range(0, prod, dn):
+        o = dot(left, rmat[:, d0 * tcols : (d0 + dn) * tcols]).astype(BF)
+        cols = [
+            jnp.concatenate(
+                [
+                    o[r * prod : (r + 1) * prod, d * tcols : (d + 1) * tcols]
+                    for d in range(dn)
+                ],
+                axis=0,
+            )
+            for r in range(pack)
+        ]
+        part = dot(wmat[:, d0 * prod : (d0 + dn) * prod], jnp.concatenate(cols, axis=1))
+        total = part if total is None else total + part
+    mid = jnp.concatenate(
+        [pair_ref[r] + total[:, r * tcols : (r + 1) * tcols].T for r in range(pack)], axis=0
+    )
+    h = (center(mid) * g_ref[...]).astype(BF)
+    spread = jnp.maximum(dot(h, widen_ref[...]), 0.0).astype(BF)
+    out = mid + dot(spread, shrink_ref[...])
+    out_ref[...] = out.reshape(out_ref.shape)
+
+
+def row_kernel(
+    heads,
+    normed_ref,
+    bias_ref,
+    x_ref,
+    wq_ref,
+    wk_ref,
+    wv_ref,
+    wo_ref,
+    g_ref,
+    widen_ref,
+    shrink_ref,
+    out_ref,
+    bmat,
+):
+    cols, srows, res, feat = normed_ref.shape
+    n, _, _, trows, tcols = bias_ref.shape
+    dim = feat // heads
+    me = lax.axis_index("col")
+
+    @pl.when(pl.program_id(0) == 0)
+    def _():
+        for k in range(n):
+            for c in range(cols):
+                bmat[:, k * trows : (k + 1) * trows, c * tcols : (c + 1) * tcols] = (
+                    bias_ref[k, c].astype(F32) * LOG2E
+                )
+
+    scale = LOG2E / dim**0.5
+    lane = lax.broadcasted_iota(jnp.int32, (res, feat), 1) // dim
+    mixed = []
+    for s in range(srows):
+        every = jnp.concatenate([normed_ref[c, s] for c in range(cols)], axis=0)
+        q = dot(normed_ref[me, s], wq_ref[...]).astype(BF)
+        key = dot(every, wk_ref[...]).astype(BF)
+        value = dot(every, wv_ref[...]).astype(BF)
+        acc = None
+        for h in range(heads):
+            qh = jnp.where(lane == h, q, jnp.zeros_like(q))
+            logit = dot(qh, key, 1, 1) * scale + bmat[h]
+            e = jnp.exp2(logit - jnp.max(logit, axis=-1, keepdims=True))
+            w = (e * (1.0 / jnp.sum(e, axis=-1, keepdims=True))).astype(BF)
+            o = dot(w, value)
+            acc = o if acc is None else jnp.where(lane == h, o, acc)
+        mixed.append(acc.astype(BF))
+    mixed = jnp.concatenate(mixed, axis=0)
+    mid = x_ref[...].reshape(srows * res, feat) + dot(mixed, wo_ref[...])
+    y = (center(mid) * g_ref[...]).astype(BF)
+    lifted = jnp.maximum(dot(y, widen_ref[...]), 0.0).astype(BF)
+    out = mid + dot(lifted, shrink_ref[...])
+    out_ref[...] = out.reshape(out_ref.shape)
+
+
+def on_device(tiles, cols, *args):
+    (x, pair, gm, gb, gf, gp, gg, bmap, wq, wk, wv, wo, widen, shrink, wl, wr, wp, gwiden, gshrink) = args
+    _, rows, res, feat = x.shape
+    _, trows, tcols, cz = pair.shape
+    heads = bmap.shape[1]
+    prod = wl.shape[1]
+    aligned = (
+        tiles % cols == 0
+        and trows * (tiles // cols) == res
+        and rows % 16 == 0
+        and trows % 16 == 0
+        and tcols % LANES == 0
+        and res % LANES == 0
+        and feat % LANES == 0
+        and cz % LANES == 0
+        and LANES % prod == 0
+    )
+    if not aligned:
+        return plain_device(*args)
+    n = tiles // cols
+    pack = LANES // prod
+    vm = pl.BlockSpec(memory_space=pltpu.VMEM)
+    dma = pltpu.SemaphoreType.DMA
+    sds = jax.ShapeDtypeStruct
+    normed, left, right, bias = pl.pallas_call(
+        functools.partial(exchange_kernel, tiles, cols),
+        out_shape=(
+            sds((cols, rows, res, feat), BF),
+            sds((tiles, trows // pack, rows, LANES), BF),
+            sds((tiles, prod, rows, tcols), BF),
+            sds((n, cols, heads, trows, tcols), BF),
+        ),
+        in_specs=[vm] * 8,
+        out_specs=(vm,) * 4,
+        scratch_shapes=[
+            pltpu.VMEM((feat // LANES, rows, res, LANES), F32),
+            pltpu.VMEM((res // pack, rows, LANES), BF),
+            pltpu.VMEM((heads, trows, tcols), BF),
+            pltpu.VMEM((pack, LANES, feat), BF),
+            dma((cols,)),
+            dma((cols,)),
+            dma((n * cols,)),
+            dma((tiles,)),
+            dma((tiles,)),
+            dma((tiles,)),
+            dma((tiles,)),
+            dma((n * cols,)),
+        ],
+        compiler_params=pltpu.CompilerParams(
+            collective_id=0, has_side_effects=True, vmem_limit_bytes=48 << 20
+        ),
+    )(x[0], pair[0], gm[None], gp[None], gb[None], bmap.T, wl.T, wr.T)
+
+    def whole(a):
+        return pl.BlockSpec(a.shape, lambda i: (0,) * a.ndim)
+
+    gg2, gf2 = gg[None], gf[None]
+    depth = rows * tiles
+    grid_revised = pl.pallas_call(
+        functools.partial(pair_kernel, depth),
+        grid=(trows // pack,),
+        out_shape=sds((trows, tcols, cz), F32),
+        in_specs=[
+            pl.BlockSpec((tiles, 1, rows, LANES), lambda i: (0, i, 0, 0)),
+            whole(right),
+            pl.BlockSpec((pack, tcols, cz), lambda i: (i, 0, 0)),
+            whole(wp),
+            whole(gg2),
+            whole(gwiden),
+            whole(gshrink),
+        ],
+        out_specs=pl.BlockSpec((pack, tcols, cz), lambda i: (i, 0, 0)),
+        scratch_shapes=[
+            pltpu.VMEM((depth, prod * tcols), BF),
+            pltpu.VMEM((cz, prod * prod), BF),
+        ],
+        compiler_params=pltpu.CompilerParams(vmem_limit_bytes=48 << 20),
+    )(left, right, pair[0], wp, gg2, gwiden, gshrink)
+
+    srows = 2
+    alignment_revised = pl.pallas_call(
+        functools.partial(row_kernel, heads),
+        grid=(rows // srows,),
+        out_shape=sds((rows, res, feat), F32),
+        in_specs=[
+            pl.BlockSpec((cols, srows, res, feat), lambda i: (0, i, 0, 0)),
+            whole(bias),
+            pl.BlockSpec((srows, res, feat), lambda i: (i, 0, 0)),
+            whole(wq),
+            whole(wk),
+            whole(wv),
+            whole(wo),
+            whole(gf2),
+            whole(widen),
+            whole(shrink),
+        ],
+        out_specs=pl.BlockSpec((srows, res, feat), lambda i: (i, 0, 0)),
+        scratch_shapes=[pltpu.VMEM((heads, res, res * cols), F32)],
+        compiler_params=pltpu.CompilerParams(vmem_limit_bytes=48 << 20),
+    )(normed, bias, x[0], wq, wk, wv, wo, gf2, widen, shrink)
+    return alignment_revised[None], grid_revised[None]
+
+
 def solution(mesh):
     placed = (
         P(("groups", "branch"), "tile", "col", None),
@@ -160,7 +611,7 @@
         P(),
     )
     return jax.shard_map(
-        on_device,
+        functools.partial(on_device, mesh.shape["tile"], mesh.shape["col"]),
         mesh=mesh,
         in_specs=placed,
         out_specs=(

time: 223 us -> 136 us (0.61)
  the two profiles are of different devices: /device:TPU:8 before, /device:TPU:10 now
where the time goes in v1:
time: 136 us; the launch traced here: 135 us
  Pallas kernels  129 us (95%)
  local copies, waits for them, and re-layouts  5.78 us (4%)
    pallas_call x1, Pallas kernels, on_device(): pl.pallas_call(functools.partial(row_kernel, heads), grid=(rows // srows,...  55.6 us
    pallas_call x1, Pallas kernels, on_device(): pl.pallas_call(functools.partial(exchange_kernel, tiles, cols), out_shape...  43.5 us
    pallas_call x1, Pallas kernels, on_device(): pl.pallas_call(functools.partial(pair_kernel, depth), grid=(trows // pack...  29.6 us
    unnamed x38, local copies, waits for them, and re-layouts  5.78 us

profile of v1, /device:TPU:10, one launch (start us, length us, event | category | flops | bytes accessed | tf_op | source)
XLA Modules:
  0.0 135.3 jit_solution(17018759125695703546)
XLA Ops:
  0.6 0.0 copy-start.1
  0.6 1.6 %copy-done.1 = f32[1,16,128,256]{3,2,1,0:T(8,128)S(1)} copy-done((f32[1,16,128,256]{3,2,1,0:T(8,128)S(1)}, f32[1,16,128,256]{3,2,1,0:T(8,128)}, u32[]{:S(2)}) %copy-start.1) | copy-done | bytes 2097176
  2.2 0.7 copy-done.11
  3.0 0.7 copy-done.12
  3.7 0.7 copy-done.13
  4.4 0.7 copy-done.15
  5.0 0.7 copy-done.16
  5.7 0.7 copy-done.18
  6.4 43.5 %shard_map.194 = (bf16[2,16,128,256]{3,2,1,0:T(8,128)(2,1)S(1)}, bf16[4,16,16,128]{3,2,1,0:T(8,128)(2,1)S(1)}, bf16[4,32,16,128]{3,2,1,0:T(8,128)(2,1)S(1)}, bf16[2,2,8,64,128]{4,3,2,1,0:T(8,128)(2,1)S(1)}) custom-call(f32[16,128,256]{2,1,0:T(8,128)S(1)} %bitcast.15, f32[64,128,128]{2,1,0:T(8,128)} %bitcast.12, f32[1,256]{1,0:T(1,128)S(1)} %bitcast.20, ...), custom_call_target="tpu_custom_call" | custom-call | tf_op jit(solution)/shard_map/pallas_call | solution.py:512
  50.0 0.0 copy-done.2
  50.0 0.0 copy-done.3
  50.0 0.0 copy-done.5
  50.0 0.0 copy-done.6
  50.0 0.0 copy-done.7
  50.0 0.0 copy-done.8
  50.0 0.0 copy-done.14
  50.0 0.0 copy-start
  50.0 0.0 copy-start.4
  50.1 0.0 copy-start.9
  50.1 0.0 copy-start.10
  50.1 0.0 copy-start.17
  50.1 55.6 %shard_map.195 = f32[16,128,256]{2,1,0:T(8,128)} custom-call(bf16[2,16,128,256]{3,2,1,0:T(8,128)(2,1)S(1)} %get-tuple-element.6.normed_ref, bf16[2,2,8,64,128]{4,3,2,1,0:T(8,128)(2,1)S(1)} %get-tuple-element.7.bias_ref, f32[16,128,256]{2,1,0:T(8,128)} %bitcast.14, bf16[256,256]{1,0:T(8,128)(2,1)S(1)} %copy-done.5, bf16[256,256]{1,0:T(8,128)(2,1)S(1)} %copy-done.6, ...), custom_call_target="tpu_custom_call" | custom-call | tf_op jit(solution)/shard_map/pallas_call | solution.py:568
  105.7 0.0 copy-done.4
  105.7 29.6 %shard_map.196 = f32[64,128,128]{2,1,0:T(8,128)} custom-call(bf16[4,16,16,128]{3,2,1,0:T(8,128)(2,1)S(1)} %get-tuple-element.8.left_ref, bf16[4,32,16,128]{3,2,1,0:T(8,128)(2,1)S(1)} %get-tuple-element.9.right_ref, f32[64,128,128]{2,1,0:T(8,128)S(1)} %bitcast.13, f32[1024,128]{1,0:T(8,128)S(1)} %copy-done.4, f32[1,128]{1,0:T(1,128)S(1)} %bitcast.22, ...), custom_call_target="tpu_custom_call" | custom-call | tf_op jit(solution)/shard_map/pallas_call | solution.py:546
  (17 shorter events, 0.0 us)
Async XLA Ops:
  0.6 1.6 %copy-start.1 = (f32[1,16,128,256]{3,2,1,0:T(8,128)S(1)}, f32[1,16,128,256]{3,2,1,0:T(8,128)}, u32[]{:S(2)}) copy-start(f32[1,16,128,256]{3,2,1,0:T(8,128)} %param.19) | copy-start | bytes 6291460
  2.2 0.7 copy-start.11
  2.9 0.7 copy-start.12
  3.7 0.7 copy-start.13
  4.4 0.7 copy-start.15
  5.0 0.7 copy-start.16
  5.7 0.7 copy-start.18
  6.4 43.6 %copy-start.2 = (bf16[256,1024]{1,0:T(8,128)(2,1)S(1)}, bf16[256,1024]{1,0:T(8,128)(2,1)}, u32[]{:S(2)}) copy-start(bf16[256,1024]{1,0:T(8,128)(2,1)} %widen_ref.2) | copy-start | bytes 1572868
  6.4 43.6 %copy-start.3 = (bf16[1024,256]{1,0:T(8,128)(2,1)S(1)}, bf16[1024,256]{1,0:T(8,128)(2,1)}, u32[]{:S(2)}) copy-start(bf16[1024,256]{1,0:T(8,128)(2,1)} %shrink_ref.2) | copy-start | bytes 1572868
  6.4 43.6 %copy-start.5 = (bf16[256,256]{1,0:T(8,128)(2,1)S(1)}, bf16[256,256]{1,0:T(8,128)(2,1)}, u32[]{:S(2)}) copy-start(bf16[256,256]{1,0:T(8,128)(2,1)} %wq_ref.1) | copy-start | bytes 393220
  6.4 43.6 %copy-start.6 = (bf16[256,256]{1,0:T(8,128)(2,1)S(1)}, bf16[256,256]{1,0:T(8,128)(2,1)}, u32[]{:S(2)}) copy-start(bf16[256,256]{1,0:T(8,128)(2,1)} %wk_ref.1) | copy-start | bytes 393220
  6.4 43.6 %copy-start.7 = (bf16[256,256]{1,0:T(8,128)(2,1)S(1)}, bf16[256,256]{1,0:T(8,128)(2,1)}, u32[]{:S(2)}) copy-start(bf16[256,256]{1,0:T(8,128)(2,1)} %wv_ref.1) | copy-start | bytes 393220
  6.4 43.6 %copy-start.8 = (bf16[256,256]{1,0:T(8,128)(2,1)S(1)}, bf16[256,256]{1,0:T(8,128)(2,1)}, u32[]{:S(2)}) copy-start(bf16[256,256]{1,0:T(8,128)(2,1)} %wo_ref.1) | copy-start | bytes 393220
  6.4 43.6 %copy-start.14 = (f32[256]{0:T(256)S(1)}, f32[256]{0:T(256)}, u32[]{:S(2)}) copy-start(f32[256]{0:T(256)} %param.23) | copy-start | bytes 3076
  50.0 55.7 %copy-start = (f32[1,64,128,128]{3,2,1,0:T(8,128)S(1)}, f32[1,64,128,128]{3,2,1,0:T(8,128)}, u32[]{:S(2)}) copy-start(f32[1,64,128,128]{3,2,1,0:T(8,128)} %param.20) | copy-start | bytes 12582916
  50.0 55.7 %copy-start.4 = (f32[1024,128]{1,0:T(8,128)S(1)}, f32[1024,128]{1,0:T(8,128)}, u32[]{:S(2)}) copy-start(f32[1024,128]{1,0:T(8,128)} %wp_ref.1) | copy-start | bytes 1572868
  50.1 55.6 %copy-start.9 = (bf16[128,512]{1,0:T(8,128)(2,1)S(1)}, bf16[128,512]{1,0:T(8,128)(2,1)}, u32[]{:S(2)}) copy-start(bf16[128,512]{1,0:T(8,128)(2,1)} %widen_ref.3) | copy-start | bytes 393220
  50.1 55.6 %copy-start.10 = (bf16[512,128]{1,0:T(8,128)(2,1)S(1)}, bf16[512,128]{1,0:T(8,128)(2,1)}, u32[]{:S(2)}) copy-start(bf16[512,128]{1,0:T(8,128)(2,1)} %shrink_ref.3) | copy-start | bytes 393220
  50.1 55.6 %copy-start.17 = (f32[128]{0:T(128)S(1)}, f32[128]{0:T(128)}, u32[]{:S(2)}) copy-start(f32[128]{0:T(128)} %param.25) | copy-start | bytes 1540

commit v2 on v1

--- a/solution.py
+++ b/solution.py
@@ -169,14 +169,21 @@
     mapt_ref,
     wlt_ref,
     wrt_ref,
+    wp_ref,
+    g_ref,
+    widen_ref,
+    shrink_ref,
     normed_ref,
     left_ref,
     right_ref,
     bias_ref,
+    out_ref,
     y_ref,
     lmine,
     bmine,
     wl4,
+    rmat,
+    wmat,
     send_x,
     recv_x,
     send_l,
@@ -348,6 +355,7 @@
         return carry
 
     lax.fori_loop(0, trows // ib, bias_body, 0)
+    reorder(rows * tiles, prod, wp_ref, wmat)
     biases = [bias_copy(t2) for t2 in range(tiles)]
     for copy in biases:
         start(copy)
@@ -360,6 +368,15 @@
     for dt in range(1, tiles):
         src = lax.rem(t + dt, tiles)
         arrived(right_ref.at[src], recv_r.at[src])
+
+    widen_right(right_ref, rmat)
+
+    def pair_body(m, carry):
+        pair_step(m, pack, left_ref, pair_ref, g_ref, widen_ref, shrink_ref, out_ref, rmat, wmat)
+        return carry
+
+    lax.fori_loop(0, trows // pack, pair_body, 0)
+
     for dc in range(1, cols):
         src = lax.rem(c + dc, cols)
         arrived(normed_ref.at[src], recv_x.at[src])
@@ -376,36 +393,27 @@
         finish(copy)
 
 
-def pair_kernel(
-    depth,
-    left_ref,
-    right_ref,
-    pair_ref,
-    wp_ref,
-    g_ref,
-    widen_ref,
-    shrink_ref,
-    out_ref,
-    rmat,
-    wmat,
-):
+def widen_right(right_ref, rmat):
     tiles, prod, rows, tcols = right_ref.shape
-    cz = pair_ref.shape[-1]
-    pack = pair_ref.shape[0]
-
-    @pl.when(pl.program_id(0) == 0)
-    def _():
-        for d in range(prod):
-            for t in range(tiles):
-                rmat[t * rows : (t + 1) * rows, d * tcols : (d + 1) * tcols] = right_ref[t, d]
-        step = LANES // prod
-        for d0 in range(0, prod, step):
-            w = jnp.concatenate(
-                [wp_ref[pl.ds(d, prod, stride=prod), :] for d in range(d0, d0 + step)], axis=0
-            )
-            wmat[:, d0 * prod : (d0 + step) * prod] = (w.T * (1.0 / depth)).astype(BF)
-
-    left = jnp.concatenate([left_ref[t, 0] for t in range(tiles)], axis=0)
+    for d in range(prod):
+        for t in range(tiles):
+            rmat[t * rows : (t + 1) * rows, d * tcols : (d + 1) * tcols] = right_ref[t, d]
+
+
+def reorder(depth, prod, wp_ref, wmat):
+    step = LANES // prod
+    for d0 in range(0, prod, step):
+        w = jnp.concatenate(
+            [wp_ref[pl.ds(d, prod, stride=prod), :] for d in range(d0, d0 + step)], axis=0
+        )
+        wmat[:, d0 * prod : (d0 + step) * prod] = (w.T * (1.0 / depth)).astype(BF)
+
+
+def pair_step(m, pack, left_ref, pair_ref, g_ref, widen_ref, shrink_ref, out_ref, rmat, wmat):
+    tiles = left_ref.shape[0]
+    _, tcols, cz = pair_ref.shape
+    prod = LANES // pack
+    left = jnp.concatenate([left_ref[t, m] for t in range(tiles)], axis=0)
     left = left.astype(F32).T.astype(BF)
     dn = 8
     total = None
@@ -424,12 +432,13 @@
         part = dot(wmat[:, d0 * prod : (d0 + dn) * prod], jnp.concatenate(cols, axis=1))
         total = part if total is None else total + part
     mid = jnp.concatenate(
-        [pair_ref[r] + total[:, r * tcols : (r + 1) * tcols].T for r in range(pack)], axis=0
+        [pair_ref[m * pack + r] + total[:, r * tcols : (r + 1) * tcols].T for r in range(pack)],
+        axis=0,
     )
     h = (center(mid) * g_ref[...]).astype(BF)
     spread = jnp.maximum(dot(h, widen_ref[...]), 0.0).astype(BF)
     out = mid + dot(spread, shrink_ref[...])
-    out_ref[...] = out.reshape(out_ref.shape)
+    out_ref[pl.ds(m * pack, pack)] = out.reshape(pack, tcols, cz)
 
 
 def row_kernel(
@@ -456,27 +465,38 @@
     def _():
         for k in range(n):
             for c in range(cols):
-                bmat[:, k * trows : (k + 1) * trows, c * tcols : (c + 1) * tcols] = (
-                    bias_ref[k, c].astype(F32) * LOG2E
-                )
+                for h in range(heads):
+                    row = h * res + k * trows
+                    bmat[row : row + trows, c * tcols : (c + 1) * tcols] = (
+                        bias_ref[k, c, h].astype(F32) * LOG2E
+                    )
 
     scale = LOG2E / dim**0.5
     lane = lax.broadcasted_iota(jnp.int32, (res, feat), 1) // dim
+    some = LANES // dim
+    local = lax.broadcasted_iota(jnp.int32, (res, LANES), 1) // dim
+    ones = jnp.ones((res * cols, LANES), BF)
     mixed = []
     for s in range(srows):
         every = jnp.concatenate([normed_ref[c, s] for c in range(cols)], axis=0)
         q = dot(normed_ref[me, s], wq_ref[...]).astype(BF)
         key = dot(every, wk_ref[...]).astype(BF)
         value = dot(every, wv_ref[...]).astype(BF)
-        acc = None
-        for h in range(heads):
-            qh = jnp.where(lane == h, q, jnp.zeros_like(q))
-            logit = dot(qh, key, 1, 1) * scale + bmat[h]
-            e = jnp.exp2(logit - jnp.max(logit, axis=-1, keepdims=True))
-            w = (e * (1.0 / jnp.sum(e, axis=-1, keepdims=True))).astype(BF)
-            o = dot(w, value)
-            acc = o if acc is None else jnp.where(lane == h, o, acc)
-        mixed.append(acc.astype(BF))
+        groups = []
+        for h0 in range(0, heads, some):
+            qs = jnp.concatenate(
+                [jnp.where(lane == h, q, jnp.zeros_like(q)) for h in range(h0, h0 + some)], axis=0
+            )
+            logit = dot(qs, key, 1, 1) * scale + bmat[h0 * res : (h0 + some) * res, :]
+            e = jnp.exp2(logit - jnp.max(logit, axis=-1, keepdims=True)).astype(BF)
+            o = dot(e, jnp.concatenate([value[:, h0 * dim : (h0 + some) * dim], ones], axis=1))
+            top = o[:res, :LANES]
+            low = o[:res, LANES:]
+            for k in range(1, some):
+                top = jnp.where(local == k, o[k * res : (k + 1) * res, :LANES], top)
+                low = jnp.where(local == k, o[k * res : (k + 1) * res, LANES:], low)
+            groups.append((top / low).astype(BF))
+        mixed.append(jnp.concatenate(groups, axis=1))
     mixed = jnp.concatenate(mixed, axis=0)
     mid = x_ref[...].reshape(srows * res, feat) + dot(mixed, wo_ref[...])
     y = (center(mid) * g_ref[...]).astype(BF)
@@ -501,6 +521,8 @@
         and feat % LANES == 0
         and cz % LANES == 0
         and LANES % prod == 0
+        and LANES % (feat // heads) == 0
+        and rows % 2 == 0
     )
     if not aligned:
         return plain_device(*args)
@@ -509,21 +531,24 @@
     vm = pl.BlockSpec(memory_space=pltpu.VMEM)
     dma = pltpu.SemaphoreType.DMA
     sds = jax.ShapeDtypeStruct
-    normed, left, right, bias = pl.pallas_call(
+    normed, left, right, bias, grid_revised = pl.pallas_call(
         functools.partial(exchange_kernel, tiles, cols),
         out_shape=(
             sds((cols, rows, res, feat), BF),
             sds((tiles, trows // pack, rows, LANES), BF),
             sds((tiles, prod, rows, tcols), BF),
             sds((n, cols, heads, trows, tcols), BF),
+            sds((trows, tcols, cz), F32),
         ),
-        in_specs=[vm] * 8,
-        out_specs=(vm,) * 4,
+        in_specs=[vm] * 12,
+        out_specs=(vm,) * 5,
         scratch_shapes=[
             pltpu.VMEM((feat // LANES, rows, res, LANES), F32),
             pltpu.VMEM((res // pack, rows, LANES), BF),
             pltpu.VMEM((heads, trows, tcols), BF),
             pltpu.VMEM((pack, LANES, feat), BF),
+            pltpu.VMEM((rows * tiles, prod * tcols), BF),
+            pltpu.VMEM((cz, prod * prod), BF),
             dma((cols,)),
             dma((cols,)),
             dma((n * cols,)),
@@ -536,34 +561,12 @@
         compiler_params=pltpu.CompilerParams(
             collective_id=0, has_side_effects=True, vmem_limit_bytes=48 << 20
         ),
-    )(x[0], pair[0], gm[None], gp[None], gb[None], bmap.T, wl.T, wr.T)
+    )(x[0], pair[0], gm[None], gp[None], gb[None], bmap.T, wl.T, wr.T, wp, gg[None], gwiden, gshrink)
 
     def whole(a):
         return pl.BlockSpec(a.shape, lambda i: (0,) * a.ndim)
 
-    gg2, gf2 = gg[None], gf[None]
-    depth = rows * tiles
-    grid_revised = pl.pallas_call(
-        functools.partial(pair_kernel, depth),
-        grid=(trows // pack,),
-        out_shape=sds((trows, tcols, cz), F32),
-        in_specs=[
-            pl.BlockSpec((tiles, 1, rows, LANES), lambda i: (0, i, 0, 0)),
-            whole(right),
-            pl.BlockSpec((pack, tcols, cz), lambda i: (i, 0, 0)),
-            whole(wp),
-            whole(gg2),
-            whole(gwiden),
-            whole(gshrink),
-        ],
-        out_specs=pl.BlockSpec((pack, tcols, cz), lambda i: (i, 0, 0)),
-        scratch_shapes=[
-            pltpu.VMEM((depth, prod * tcols), BF),
-            pltpu.VMEM((cz, prod * prod), BF),
-        ],
-        compiler_params=pltpu.CompilerParams(vmem_limit_bytes=48 << 20),
-    )(left, right, pair[0], wp, gg2, gwiden, gshrink)
-
+    gf2 = gf[None]
     srows = 2
     alignment_revised = pl.pallas_call(
         functools.partial(row_kernel, heads),
@@ -582,7 +585,7 @@
             whole(shrink),
         ],
         out_specs=pl.BlockSpec((srows, res, feat), lambda i: (i, 0, 0)),
-        scratch_shapes=[pltpu.VMEM((heads, res, res * cols), F32)],
+        scratch_shapes=[pltpu.VMEM((heads * res, res * cols), F32)],
         compiler_params=pltpu.CompilerParams(vmem_limit_bytes=48 << 20),
     )(normed, bias, x[0], wq, wk, wv, wo, gf2, widen, shrink)
     return alignment_revised[None], grid_revised[None]

time: 136 us -> 103 us (0.76)
  the two profiles are of different devices: /device:TPU:10 before, /device:TPU:8 now
where the time goes in v2:
time: 103 us
  Pallas kernels  92.3 us (90%)
  local copies, waits for them, and re-layouts  9.76 us (9%)
    pallas_call x1, Pallas kernels, on_device(): pl.pallas_call(functools.partial(exchange_kernel, tiles, cols), out_shape...  70.1 us
    pallas_call x1, Pallas kernels, on_device(): pl.pallas_call(functools.partial(row_kernel, heads), grid=(rows // srows,...  22.3 us
    unnamed x37, local copies, waits for them, and re-layouts  9.76 us

profile of v2, /device:TPU:8, one launch (start us, length us, event | category | flops | bytes accessed | tf_op | source)
XLA Modules:
  0.0 102.8 jit_solution(13530928262414088621)
XLA Ops:
  0.6 0.0 copy-start.1
  0.6 0.0 copy-start
  0.7 0.0 copy-start.2
  0.7 1.1 %copy-done.2 = f32[1024,128]{1,0:T(8,128)S(1)} copy-done((f32[1024,128]{1,0:T(8,128)S(1)}, f32[1024,128]{1,0:T(8,128)}, u32[]{:S(2)}) %copy-start.2) | copy-done | bytes 524312
  1.8 0.9 copy-done.7
  2.7 0.9 copy-done.8
  3.6 0.7 copy-done.9
  4.3 0.7 copy-done.10
  5.0 0.7 copy-done.11
  5.7 0.7 copy-done.13
  6.4 0.7 copy-done.14
  7.1 0.7 copy-done.15
  7.7 0.7 copy-done.16
  8.4 0.0 copy-start.12
  8.4 70.1 %shard_map.194 = (bf16[2,16,128,256]{3,2,1,0:T(8,128)(2,1)S(1)}, bf16[4,16,16,128]{3,2,1,0:T(8,128)(2,1)}, bf16[4,32,16,128]{3,2,1,0:T(8,128)(2,1)}, bf16[2,2,8,...) custom-call(f32[16,128,256]{2,1,0:T(8,128)} %bitcast.20, f32[64,128,128]{2,1,0:T(8,128)} %bitcast.22, f32[1,256]{1,0:T(1,128)S(1)} %bitcast.16, ...), custom_call_target="tpu_custom_call" | custom-call | tf_op jit(solution)/shard_map/pallas_call | solution.py:534
  78.5 0.0 copy-done.1
  78.5 0.0 copy-done
  78.5 0.0 copy-done.3
  78.5 0.0 copy-done.4
  78.5 0.0 copy-done.5
  78.5 0.0 copy-done.6
  78.5 0.0 copy-done.12
  78.6 22.3 %shard_map.195 = f32[16,128,256]{2,1,0:T(8,128)} custom-call(bf16[2,16,128,256]{3,2,1,0:T(8,128)(2,1)S(1)} %get-tuple-element.5.normed_ref, bf16[2,2,8,64,128]{4,3,2,1,0:T(8,128)(2,1)S(1)} %get-tuple-element.6.bias_ref, f32[16,128,256]{2,1,0:T(8,128)} %bitcast.21, bf16[256,256]{1,0:T(8,128)(2,1)S(1)} %copy-done.3, bf16[256,256]{1,0:T(8,128)(2,1)S(1)} %copy-done.4, ...), custom_call_target="tpu_custom_call" | custom-call | tf_op jit(solution)/shard_map/pallas_call | solution.py:571
  100.8 2.0 %copy.22 = f32[1,64,128,128]{3,2,1,0:T(8,128)} copy(f32[1,64,128,128]{3,2,1,0:T(8,128)S(1)} %bitcast.23) | data formatting | bytes 8388608
  (15 shorter events, 0.0 us)
Async XLA Ops:
  0.6 77.8 %copy-start.1 = (bf16[1024,256]{1,0:T(8,128)(2,1)S(1)}, bf16[1024,256]{1,0:T(8,128)(2,1)}, u32[]{:S(2)}) copy-start(bf16[1024,256]{1,0:T(8,128)(2,1)} %shrink_ref.3) | copy-start | bytes 1572868
  0.6 77.8 %copy-start = (bf16[256,1024]{1,0:T(8,128)(2,1)S(1)}, bf16[256,1024]{1,0:T(8,128)(2,1)}, u32[]{:S(2)}) copy-start(bf16[256,1024]{1,0:T(8,128)(2,1)} %widen_ref.3) | copy-start | bytes 1572868
  0.7 1.1 %copy-start.2 = (f32[1024,128]{1,0:T(8,128)S(1)}, f32[1024,128]{1,0:T(8,128)}, u32[]{:S(2)}) copy-start(f32[1024,128]{1,0:T(8,128)} %wp_ref.1) | copy-start | bytes 1572868
  1.8 0.9 copy-start.7
  2.7 0.9 copy-start.8
  3.6 0.7 copy-start.9
  4.3 0.7 copy-start.10
  5.0 0.7 copy-start.11
  5.7 0.7 copy-start.13
  6.4 0.7 copy-start.14
  7.1 0.7 copy-start.15
  7.7 0.7 copy-start.16
  8.4 70.1 %copy-start.3 = (bf16[256,256]{1,0:T(8,128)(2,1)S(1)}, bf16[256,256]{1,0:T(8,128)(2,1)}, u32[]{:S(2)}) copy-start(bf16[256,256]{1,0:T(8,128)(2,1)} %wq_ref.1) | copy-start | bytes 393220
  8.4 70.1 %copy-start.4 = (bf16[256,256]{1,0:T(8,128)(2,1)S(1)}, bf16[256,256]{1,0:T(8,128)(2,1)}, u32[]{:S(2)}) copy-start(bf16[256,256]{1,0:T(8,128)(2,1)} %wk_ref.1) | copy-start | bytes 393220
  8.4 70.1 %copy-start.5 = (bf16[256,256]{1,0:T(8,128)(2,1)S(1)}, bf16[256,256]{1,0:T(8,128)(2,1)}, u32[]{:S(2)}) copy-start(bf16[256,256]{1,0:T(8,128)(2,1)} %wv_ref.1) | copy-start | bytes 393220
  8.4 70.1 %copy-start.6 = (bf16[256,256]{1,0:T(8,128)(2,1)S(1)}, bf16[256,256]{1,0:T(8,128)(2,1)}, u32[]{:S(2)}) copy-start(bf16[256,256]{1,0:T(8,128)(2,1)} %wo_ref.1) | copy-start | bytes 393220
  8.4 70.1 %copy-start.12 = (f32[256]{0:T(256)S(1)}, f32[256]{0:T(256)}, u32[]{:S(2)}) copy-start(f32[256]{0:T(256)} %param.23) | copy-start | bytes 3076
  78.5 22.3 %copy-start.17 = (f32[64,128,128]{2,1,0:T(8,128)S(1)}, f32[64,128,128]{2,1,0:T(8,128)}, u32[]{:S(2)}) copy-start(f32[64,128,128]{2,1,0:T(8,128)} %get-tuple-element.7) | copy-start | bytes 12582916

commit v3 on v2

--- a/solution.py
+++ b/solution.py
@@ -235,7 +235,7 @@
         own[s, :, :] = (z * gm).astype(BF)
         return carry
 
-    lax.fori_loop(0, rows, rows_body, 0)
+    lax.fori_loop(0, rows, rows_body, 0, unroll=2)
 
     group = 16
     for s0 in range(0, rows, group):
@@ -333,8 +333,6 @@
         start(copy)
     for dt in range(1, tiles):
         right_copy(dt).start()
-    for dc in range(1, cols):
-        normed_copy(dc).start()
 
     mapt = mapt_ref[...] * gb_ref[...]
     high = mapt.astype(BF)
@@ -357,9 +355,6 @@
     lax.fori_loop(0, trows // ib, bias_body, 0)
     reorder(rows * tiles, prod, wp_ref, wmat)
     biases = [bias_copy(t2) for t2 in range(tiles)]
-    for copy in biases:
-        start(copy)
-
     def arrived(ref, sem):
         pltpu.make_async_copy(ref, ref, sem).wait()
 
@@ -368,6 +363,10 @@
     for dt in range(1, tiles):
         src = lax.rem(t + dt, tiles)
         arrived(right_ref.at[src], recv_r.at[src])
+    for copy in biases:
+        start(copy)
+    for dc in range(1, cols):
+        normed_copy(dc).start()
 
     widen_right(right_ref, rmat)
 
@@ -375,7 +374,7 @@
         pair_step(m, pack, left_ref, pair_ref, g_ref, widen_ref, shrink_ref, out_ref, rmat, wmat)
         return carry
 
-    lax.fori_loop(0, trows // pack, pair_body, 0)
+    lax.fori_loop(0, trows // pack, pair_body, 0, unroll=2)
 
     for dc in range(1, cols):
         src = lax.rem(c + dc, cols)

time: 103 us -> 100 us (0.971)
  Pallas kernels: 92.3 us -> 89.5 us
    pallas_call x1, Pallas kernels: 70.1 us -> 67.2 us  [on_device(): pl.pallas_call(functools.partial(exchange_kernel, tiles, cols), out_shape...]
where the time goes in v3:
time: 100 us
  Pallas kernels  89.5 us (90%)
  local copies, waits for them, and re-layouts  9.76 us (10%)
    pallas_call x1, Pallas kernels, on_device(): pl.pallas_call(functools.partial(exchange_kernel, tiles, cols), out_shape...  67.2 us
    pallas_call x1, Pallas kernels, on_device(): pl.pallas_call(functools.partial(row_kernel, heads), grid=(rows // srows,...  22.3 us
    unnamed x37, local copies, waits for them, and re-layouts  9.76 us

profile of v3, /device:TPU:8, one launch (start us, length us, event | category | flops | bytes accessed | tf_op | source)
XLA Modules:
  0.0 100.0 jit_solution(2160075942268586065)
XLA Ops:
  0.6 0.0 copy-start.1
  0.6 0.0 copy-start
  0.7 0.0 copy-start.2
  0.7 1.1 %copy-done.2 = f32[1024,128]{1,0:T(8,128)S(1)} copy-done((f32[1024,128]{1,0:T(8,128)S(1)}, f32[1024,128]{1,0:T(8,128)}, u32[]{:S(2)}) %copy-start.2) | copy-done | bytes 524312
  1.8 0.9 copy-done.7
  2.7 0.9 copy-done.8
  3.6 0.7 copy-done.9
  4.3 0.7 copy-done.10
  5.0 0.7 copy-done.11
  5.7 0.7 copy-done.13
  6.4 0.7 copy-done.14
  7.1 0.7 copy-done.15
  7.7 0.7 copy-done.16
  8.4 0.0 copy-start.12
  8.4 67.2 %shard_map.194 = (bf16[2,16,128,256]{3,2,1,0:T(8,128)(2,1)S(1)}, bf16[4,16,16,128]{3,2,1,0:T(8,128)(2,1)}, bf16[4,32,16,128]{3,2,1,0:T(8,128)(2,1)}, bf16[2,2,8,...) custom-call(f32[16,128,256]{2,1,0:T(8,128)} %bitcast.20, f32[64,128,128]{2,1,0:T(8,128)} %bitcast.22, f32[1,256]{1,0:T(1,128)S(1)} %bitcast.16, ...), custom_call_target="tpu_custom_call" | custom-call | tf_op jit(solution)/shard_map/pallas_call | solution.py:533
  75.6 0.0 copy-done.1
  75.6 0.0 copy-done
  75.7 0.0 copy-done.3
  75.7 0.0 copy-done.4
  75.7 0.0 copy-done.5
  75.7 0.0 copy-done.6
  75.7 0.0 copy-done.12
  75.7 22.3 %shard_map.195 = f32[16,128,256]{2,1,0:T(8,128)} custom-call(bf16[2,16,128,256]{3,2,1,0:T(8,128)(2,1)S(1)} %get-tuple-element.5.normed_ref, bf16[2,2,8,64,128]{4,3,2,1,0:T(8,128)(2,1)S(1)} %get-tuple-element.6.bias_ref, f32[16,128,256]{2,1,0:T(8,128)} %bitcast.21, bf16[256,256]{1,0:T(8,128)(2,1)S(1)} %copy-done.3, bf16[256,256]{1,0:T(8,128)(2,1)S(1)} %copy-done.4, ...), custom_call_target="tpu_custom_call" | custom-call | tf_op jit(solution)/shard_map/pallas_call | solution.py:570
  98.0 2.0 %copy.22 = f32[1,64,128,128]{3,2,1,0:T(8,128)} copy(f32[1,64,128,128]{3,2,1,0:T(8,128)S(1)} %bitcast.23) | data formatting | bytes 8388608
  (15 shorter events, 0.0 us)
Async XLA Ops:
  0.6 75.0 %copy-start.1 = (bf16[1024,256]{1,0:T(8,128)(2,1)S(1)}, bf16[1024,256]{1,0:T(8,128)(2,1)}, u32[]{:S(2)}) copy-start(bf16[1024,256]{1,0:T(8,128)(2,1)} %shrink_ref.3) | copy-start | bytes 1572868
  0.6 75.0 %copy-start = (bf16[256,1024]{1,0:T(8,128)(2,1)S(1)}, bf16[256,1024]{1,0:T(8,128)(2,1)}, u32[]{:S(2)}) copy-start(bf16[256,1024]{1,0:T(8,128)(2,1)} %widen_ref.3) | copy-start | bytes 1572868
  0.7 1.1 %copy-start.2 = (f32[1024,128]{1,0:T(8,128)S(1)}, f32[1024,128]{1,0:T(8,128)}, u32[]{:S(2)}) copy-start(f32[1024,128]{1,0:T(8,128)} %wp_ref.1) | copy-start | bytes 1572868
  1.8 0.9 copy-start.7
  2.7 0.9 copy-start.8
  3.6 0.7 copy-start.9
  4.3 0.7 copy-start.10
  5.0 0.7 copy-start.11
  5.7 0.7 copy-start.13
  6.4 0.7 copy-start.14
  7.1 0.7 copy-start.15
  7.7 0.7 copy-start.16
  8.4 67.3 %copy-start.3 = (bf16[256,256]{1,0:T(8,128)(2,1)S(1)}, bf16[256,256]{1,0:T(8,128)(2,1)}, u32[]{:S(2)}) copy-start(bf16[256,256]{1,0:T(8,128)(2,1)} %wq_ref.1) | copy-start | bytes 393220
  8.4 67.3 %copy-start.4 = (bf16[256,256]{1,0:T(8,128)(2,1)S(1)}, bf16[256,256]{1,0:T(8,128)(2,1)}, u32[]{:S(2)}) copy-start(bf16[256,256]{1,0:T(8,128)(2,1)} %wk_ref.1) | copy-start | bytes 393220
  8.4 67.3 %copy-start.5 = (bf16[256,256]{1,0:T(8,128)(2,1)S(1)}, bf16[256,256]{1,0:T(8,128)(2,1)}, u32[]{:S(2)}) copy-start(bf16[256,256]{1,0:T(8,128)(2,1)} %wv_ref.1) | copy-start | bytes 393220
  8.4 67.3 %copy-start.6 = (bf16[256,256]{1,0:T(8,128)(2,1)S(1)}, bf16[256,256]{1,0:T(8,128)(2,1)}, u32[]{:S(2)}) copy-start(bf16[256,256]{1,0:T(8,128)(2,1)} %wo_ref.1) | copy-start | bytes 393220
  8.4 67.3 %copy-start.12 = (f32[256]{0:T(256)S(1)}, f32[256]{0:T(256)}, u32[]{:S(2)}) copy-start(f32[256]{0:T(256)} %param.23) | copy-start | bytes 3076
  75.7 22.3 %copy-start.17 = (f32[64,128,128]{2,1,0:T(8,128)S(1)}, f32[64,128,128]{2,1,0:T(8,128)}, u32[]{:S(2)}) copy-start(f32[64,128,128]{2,1,0:T(8,128)} %get-tuple-element.7) | copy-start | bytes 12582916
